TPU v7x, 32 devices: a whole 2x2x4 slice. The times are simulated.
32 devices in a mesh: groups: 2 (over x), blk: 8 (over z, y), rep: 2 (over core).
Axes of the slice: x: 2, y: 2, z: 4, core: 2. Of those that a mesh axis runs over, the one named last changes fastest.
Arguments:
- frames: bfloat16 [65536, 64], P(('groups', 'blk')), parts along dimension 0, may hold values from -6 to 6
- degree: float32 [65536], P(('groups', 'blk')), parts along dimension 0, may hold values from 1 to 16
- start: float32 [65536, 64], P(('groups', 'blk')), parts along dimension 0, may hold values from -6 to 6
- block_slot: int32 [64], P('groups'), parts along dimension 0, may hold values from 0 to 31, as said below
- pair_list: int32 [16, 2, 4, 2], P(('groups', 'blk'), 'rep'), parts along dimension 0, may hold values from 0 to 31, as said below
- pair_count: int32 [16, 2], P(('groups', 'blk'), 'rep'), parts along dimension 0, may hold values from 3 to 4, as said below
Outputs:
- subspace: float32 [65536, 64], P(('groups', 'blk', 'rep')), parts along dimension 0
- factor: float32 [128, 64], P('groups'), parts along dimension 0
There are 2 independent parts, one for each index of `groups`. A program takes and returns all parts, laid end to end along the dimension named above; each array names one. Nothing has to cross between parts.
Inputs may be any that keep to these rules, and one draw needn't show every extreme that they name: `block_slot`: A permutation of the 32 storage slots; slot s lies on blk index s // 4. Every row block of pair_list[i] sits at a storage slot on blk index i. Over the two halves of one owner, all 8 slots, live or not, name column blocks on different blk indices. Slots beyond pair_count are ignored. A pair may be listed more than once over all owners; each listing adds its tile. `pair_count`: counts differ from device to device.
All inputs are finite; a program needn't handle non-finite values.
Results may differ from a plain program's by a relative error of at most 0.0091.
Values may be sent and summed in bfloat16 or wider, within the bound.
A program may use at most 128 MiB of HBM per device.

v0:
```python
import jax
import jax.numpy as jnp
from jax import lax
from jax.sharding import PartitionSpec as P

BS = 1024
D_CV = 64
ITERS = 2


def gauss_tile(left, right):
    left_sq = jnp.sum(jnp.square(left.astype(jnp.float32)), axis=1)
    right_sq = jnp.sum(jnp.square(right.astype(jnp.float32)), axis=1)
    cross = lax.dot_general(
        left, right, (((1,), (1,)), ((), ())), preferred_element_type=jnp.float32
    )
    dist = left_sq[:, None] + right_sq[None, :] - 2.0 * cross
    return jnp.exp(-dist * (4.0 / D_CV)).astype(jnp.bfloat16)


def gram_of(mapped):
    return lax.dot_general(
        mapped,
        mapped,
        (((0,), (0,)), ((), ())),
        precision=lax.Precision.HIGHEST,
        preferred_element_type=jnp.float32,
    )


def per_device(frames, degree, start, block_slot, pair_list, pair_count):
    peers = lax.axis_size("blk")
    me = lax.axis_index("blk")
    rep_me = lax.axis_index("rep")
    halves = lax.axis_size("rep")
    local_rows = frames.shape[0]
    local_blocks = local_rows // BS
    width = start.shape[1]
    total_rows = local_rows * peers
    blocks_all = block_slot.shape[0]
    slots_dev = pair_list.shape[2]
    pairs = pair_list[0, 0]
    count = pair_count[0, 0]
    block_ids = jnp.arange(blocks_all, dtype=jnp.int32)

    def slot_of(ids):
        return jnp.sum(
            jnp.where(ids[:, None] == block_ids[None, :], block_slot[None, :], 0), axis=1
        )

    row_slot = slot_of(pairs[:, 0])
    col_slot = slot_of(pairs[:, 1])
    row_local = row_slot - me * local_blocks
    col_peer = col_slot // local_blocks
    col_local = col_slot - col_peer * local_blocks
    live = jnp.arange(slots_dev, dtype=jnp.int32) < count
    peer_ids = jnp.arange(peers, dtype=jnp.int32)
    wanted = jnp.max(
        jnp.where(live[None, :] & (col_peer[None, :] == peer_ids[:, None]), col_local[None, :], -1),
        axis=1,
    )
    asked = lax.all_to_all(
        wanted.reshape(peers, 1), "blk", split_axis=0, concat_axis=0, tiled=True
    )[:, 0]
    chosen = jnp.clip(asked, 0, local_blocks - 1)
    served = asked >= 0
    owner_hit = (asked[:, None] == jnp.arange(local_blocks, dtype=jnp.int32)[None, :]).astype(
        jnp.bfloat16
    )
    frame_blocks = frames.reshape(local_blocks, BS, D_CV)
    scale = lax.rsqrt(degree).reshape(local_blocks, BS, 1)
    stored_init = jnp.zeros((1, 1, 1), jnp.bfloat16)
    stored = stored_init
    scaled = (start.reshape(local_blocks, BS, width) * scale).astype(jnp.bfloat16)
    result = start
    factor = jnp.zeros((width, width), jnp.float32)
    for step in range(ITERS):
        payload = jnp.concatenate([frame_blocks, scaled], axis=2)
        outgoing = jnp.where(
            served[:, None, None], jnp.take(payload, chosen, axis=0), jnp.zeros((), payload.dtype)
        )
        arrived = lax.all_to_all(outgoing, "blk", split_axis=0, concat_axis=0, tiled=True)

        def apply_pair(index, carry):
            sums, outbox, kept = carry
            here = row_local[index]
            there = col_peer[index]
            mine_scaled = lax.dynamic_index_in_dim(scaled, here, 0, keepdims=False)
            received = lax.dynamic_index_in_dim(arrived, there, 0, keepdims=False)
            mine_frames = lax.dynamic_index_in_dim(frame_blocks, here, 0, keepdims=False)
            tile = gauss_tile(mine_frames, received[:, :D_CV])
            their_scaled = received[:, D_CV:]
            forward = jnp.dot(tile, their_scaled, preferred_element_type=jnp.float32)
            sums = sums.at[here].add(forward)
            backward = lax.dot_general(
                tile, mine_scaled, (((0,), (0,)), ((), ())), preferred_element_type=jnp.float32
            )
            backward = jnp.where(
                row_slot[index] != col_slot[index], backward, jnp.zeros_like(backward)
            ).astype(jnp.bfloat16)
            outbox = lax.dynamic_update_index_in_dim(outbox, backward, there, 0)
            return (sums, outbox, kept)

        sums_init = jnp.zeros((local_blocks, BS, width), jnp.float32)
        outbox_init = jnp.zeros((peers, BS, width), jnp.bfloat16)
        sums, outbox, stored = lax.fori_loop(0, count, apply_pair, (sums_init, outbox_init, stored))
        returned = lax.all_to_all(outbox, "blk", split_axis=0, concat_axis=0, tiled=True)
        sums = sums + jnp.einsum(
            "pb,pnk->bnk", owner_hit, returned, preferred_element_type=jnp.float32
        )
        combined = lax.psum(sums, "rep")
        mapped = (combined * scale).reshape(local_rows, width)
        gram = lax.psum(gram_of(mapped), "blk") / total_rows
        factor = jnp.linalg.cholesky(gram)
        vectors = jax.scipy.linalg.solve_triangular(factor, mapped.T, lower=True).T
        if step + 1 < ITERS:
            scaled = (vectors.reshape(local_blocks, BS, width) * scale).astype(jnp.bfloat16)
        share = local_rows // halves
        result = lax.dynamic_slice_in_dim(vectors, rep_me * share, share, 0)
    return (result, factor)


def solution(mesh):
    placed = (
        P(("groups", "blk"), None),
        P(("groups", "blk")),
        P(("groups", "blk"), None),
        P("groups"),
        P(("groups", "blk"), "rep", None, None),
        P(("groups", "blk"), "rep"),
    )
    return jax.shard_map(
        per_device,
        mesh=mesh,
        in_specs=placed,
        out_specs=(P(("groups", "blk", "rep"), None), P("groups", None)),
        check_vma=False,
    )
```

profile of v0, /device:TPU:0, one launch (start us, length us, event | category | flops | bytes accessed | tf_op | source)
XLA Modules:
  0.0 519.8 jit_solution(11157516814704794737)
XLA Ops:
  10.2 7.3 %all-to-all-start = ((s32[8,1,1]{2,1,0:T(1,128)}), s32[8,1,1]{2,1,0:T(1,128)S(1)}, u32[]{:S(2)}, u32[]{:S(2)}) async-start(s32[8,1,1]{2,1,0:T(1,128)} %copy.82), calls=%async_computation | async-start | bytes 8192 | tf_op jit(solution)/shard_map/all_to_all | solution.py:62
  18.3 1.9 reshape.143
  25.4 1.6 select_select_fusion.1
  27.0 6.1 %all-to-all-start.1 = ((bf16[8,1024,128]{2,1,0:T(8,128)(2,1)}), bf16[8,1024,128]{2,1,0:T(8,128)(2,1)}, u32[]{:S(2)}, u32[]{:S(2)}) async-start(bf16[8,1024,128]{2,1,0:T(8,128)(2,1)} %select_select_fusion.1), calls=%async_computation.1 | async-start | bytes 4194304 | tf_op jit(solution)/shard_map/all_to_all | solution.py:82
  34.6 46.3 %all-to-all-done.1 = bf16[8,1024,128]{2,1,0:T(8,128)(2,1)} async-done(((bf16[8,1024,128]{2,1,0:T(8,128)(2,1)}), bf16[8,1024,128]{2,1,0:T(8,128)(2,1)}, u32[]{:S(2)}, u32[]{:S(2)}) %all-to-all-start.1) | async-done | bytes 2097184 | tf_op jit(solution)/shard_map/all_to_all | solution.py:82
  82.2 84.0 %while.26 = (s32[]{:T(128)}, f32[4,1024,64]{1,0,2:T(4,128)S(1)}, bf16[8,1024,64]{1,2,0:T(8,128)(2,1)}, s32[]{:T(128)}, s32[4]{0:T(128)S(1)}, /*index=5*/bf16[4,1...) while((s32[]{:T(128)}, f32[4,1024,64]{1,0,2:T(4,128)S(1)}, ...), condition=%wide.region_7.9_spmd, body=%wide.region_3.8_spmd.sunk | while | flops 409597984 | bytes 19154336 | solution.py:106
  90.1 2.0 exponential_convert_fusion.4
  93.1 1.5 fusion.70
  94.8 2.1 scatter-add.12
  110.9 2.0 exponential_convert_fusion.4
  114.0 1.5 fusion.70
  115.7 2.1 scatter-add.12
  131.7 2.0 exponential_convert_fusion.4
  134.8 1.5 fusion.70
  136.5 2.1 scatter-add.12
  152.6 2.0 exponential_convert_fusion.4
  155.6 1.5 fusion.70
  157.3 2.1 scatter-add.12
  166.2 27.7 %all_to_all.29 = bf16[8,1024,64]{1,2,0:T(8,128)(2,1)S(1)} all-to-all(bf16[8,1024,64]{1,2,0:T(8,128)(2,1)} %get-tuple-element.148), channel_id=1, replica_groups=mesh['groups'=2,'blk'=8,'rep'=2] {'blk'}, dimensions={0} | all-to-all | bytes 2097152 | tf_op jit(solution)/shard_map/all_to_all | solution.py:107
  193.9 1.8 convolution_add_fusion.1
  195.8 20.6 %all-reduce.3.cloned.1.call-done = f32[4,1024,64]{1,0,2:T(4,128)} async-done(((f32[4,1024,64]{1,0,2:T(4,128)}), f32[4,1024,64]{1,0,2:T(4,128)}) %all-reduce.3.cloned.1.call-update) | async-done | bytes 1048592 | tf_op jit(solution)/shard_map/psum | solution.py:111
  217.7 2.0 convolution_bitcast_fusion.4
  219.7 37.4 %psum.29 = f32[64,64]{0,1:T(8,128)S(1)} all-reduce(f32[64,64]{0,1:T(8,128)S(1)} %convolution_bitcast_fusion.4), channel_id=1, replica_groups=mesh['groups'=2,'blk'=8,'rep'=2] {'blk'}, use_global_device_ids=true, to_apply=%region_9.11 | all-reduce | flops 4096 | bytes 32768 | tf_op jit(solution)/shard_map/psum | solution.py:113
  257.3 5.8 %cholesky.44 = f32[64,64]{1,0:T(8,128)S(1)} custom-call(f32[64,64]{1,0:T(8,128)S(1)} %fusion.33), custom_call_target="Cholesky" | custom-call | tf_op jit(solution)/shard_map/jit(cholesky)/cholesky | solution.py:114
  264.4 4.9 custom-call.6
  275.4 1.6 select_select_fusion
  277.0 4.3 all-to-all-start.3
  281.4 41.9 %all-to-all-done.3 = bf16[8,1024,128]{2,1,0:T(8,128)(2,1)} async-done(((bf16[8,1024,128]{2,1,0:T(8,128)(2,1)}), bf16[8,1024,128]{2,1,0:T(8,128)(2,1)}, u32[]{:S(2)}, u32[]{:S(2)}) %all-to-all-start.3) | async-done | bytes 2097184 | tf_op jit(solution)/shard_map/all_to_all | solution.py:82
  324.6 84.6 %while.27 = (s32[]{:T(128)}, f32[4,1024,64]{1,0,2:T(4,128)S(1)}, bf16[8,1024,64]{1,2,0:T(8,128)(2,1)}, s32[]{:T(128)}, s32[4]{0:T(128)S(1)}, /*index=5*/bf16[4,1...) while((s32[]{:T(128)}, f32[4,1024,64]{1,0,2:T(4,128)S(1)}, ...), condition=%wide.region_16.20_spmd, body=%wide.region_12.19_spmd.sunk | while | flops 409597984 | bytes 19154336 | solution.py:106
  332.6 2.0 exponential_convert_fusion.5
  335.7 1.5 fusion.78
  337.4 2.1 scatter-add.13
  353.6 2.0 exponential_convert_fusion.5
  356.6 1.5 fusion.78
  358.4 2.1 scatter-add.13
  374.6 2.0 exponential_convert_fusion.5
  377.6 1.5 fusion.78
  379.4 2.1 scatter-add.13
  395.6 2.0 exponential_convert_fusion.5
  398.6 1.5 fusion.78
  400.4 2.1 scatter-add.13
  409.2 24.7 %all_to_all.30 = bf16[8,1024,64]{1,2,0:T(8,128)(2,1)S(1)} all-to-all(bf16[8,1024,64]{1,2,0:T(8,128)(2,1)} %get-tuple-element.150), channel_id=1, replica_groups=mesh['groups'=2,'blk'=8,'rep'=2] {'blk'}, dimensions={0} | all-to-all | bytes 2097152 | tf_op jit(solution)/shard_map/all_to_all | solution.py:107
  433.9 1.8 convolution_add_fusion
  435.8 21.1 %all-reduce.5.cloned.1.call-done = f32[4,1024,64]{1,0,2:T(4,128)} async-done(((f32[4,1024,64]{1,0,2:T(4,128)}), f32[4,1024,64]{1,0,2:T(4,128)}) %all-reduce.5.cloned.1.call-update) | async-done | bytes 1048592 | tf_op jit(solution)/shard_map/psum | solution.py:111
  458.2 2.0 convolution_bitcast_fusion.3
  460.3 37.4 %psum.31 = f32[64,64]{0,1:T(8,128)S(1)} all-reduce(f32[64,64]{0,1:T(8,128)S(1)} %convolution_bitcast_fusion.3), channel_id=1, replica_groups=mesh['groups'=2,'blk'=8,'rep'=2] {'blk'}, use_global_device_ids=true, to_apply=%region_18.22 | all-reduce | flops 4096 | bytes 32768 | tf_op jit(solution)/shard_map/psum | solution.py:113
  497.8 5.8 %cholesky.55 = f32[64,64]{1,0:T(8,128)S(1)} custom-call(f32[64,64]{1,0:T(8,128)S(1)} %fusion.31), custom_call_target="Cholesky" | custom-call | tf_op jit(solution)/shard_map/jit(cholesky)/cholesky | solution.py:114
  505.6 4.9 custom-call.7
  (196 shorter events, 103.8 us)
Async XLA Ops:
  7.2 13.0 %copy-start.9 = (bf16[4096,64]{0,1:T(8,128)(2,1)S(1)}, bf16[4096,64]{0,1:T(8,128)(2,1)}, u32[]{:S(2)}) copy-start(bf16[4096,64]{0,1:T(8,128)(2,1)} %param.19) | copy-start | bytes 1572868
  10.2 13.7 %all-to-all-start = ((s32[8,1,1]{2,1,0:T(1,128)}), s32[8,1,1]{2,1,0:T(1,128)S(1)}, u32[]{:S(2)}, u32[]{:S(2)}) async-start(s32[8,1,1]{2,1,0:T(1,128)} %copy.82), calls=%async_computation | async-start | bytes 8192 | tf_op jit(solution)/shard_map/all_to_all | solution.py:62
  20.6 0.8 copy-start.6
  21.4 0.8 copy-start.4
  27.0 6.2 %copy-start.7 = (bf16[4,1024,64]{1,0,2:T(4,128)(2,1)S(1)}, bf16[4,1024,64]{1,0,2:T(4,128)(2,1)}, u32[]{:S(2)}) copy-start(bf16[4,1024,64]{1,0,2:T(4,128)(2,1)} %copy-done.6) | copy-start | bytes 1572868
  27.0 53.9 %all-to-all-start.1 = ((bf16[8,1024,128]{2,1,0:T(8,128)(2,1)}), bf16[8,1024,128]{2,1,0:T(8,128)(2,1)}, u32[]{:S(2)}, u32[]{:S(2)}) async-start(bf16[8,1024,128]{2,1,0:T(8,128)(2,1)} %select_select_fusion.1), calls=%async_computation.1 | async-start | bytes 4194304 | tf_op jit(solution)/shard_map/all_to_all | solution.py:82
  33.1 49.2 %copy-start.10 = (s32[3]{0:T(128)S(1)}, s32[3]{0:T(128)}, u32[]{:S(2)}) copy-start(s32[3]{0:T(128)} %constant.147.clone.1) | copy-start | bytes 40
  33.1 183.3 %all-reduce.3.cloned.1.call-start = ((), (), s32[]{:S(2)}) async-start(), calls=%async_computation.5 | async-start | bytes 2097152 | tf_op jit(solution)/shard_map/psum | solution.py:111
  96.9 1.0 copy-start.2
  99.5 3.6 copy-start.3
  117.8 1.0 copy-start.2
  120.3 3.6 copy-start.3
  138.6 1.0 copy-start.2
  141.1 3.6 copy-start.3
  159.4 1.0 copy-start.2
  161.9 3.6 copy-start.3
  271.0 1.8 copy-start.8
  272.0 0.8 copy-start.5
  277.0 46.3 %all-to-all-start.3 = ((bf16[8,1024,128]{2,1,0:T(8,128)(2,1)}), bf16[8,1024,128]{2,1,0:T(8,128)(2,1)}, u32[]{:S(2)}, u32[]{:S(2)}) async-start(bf16[8,1024,128]{2,1,0:T(8,128)(2,1)} %select_select_fusion), calls=%async_computation.3 | async-start | bytes 4194304 | tf_op jit(solution)/shard_map/all_to_all | solution.py:82
  281.3 175.6 %all-reduce.5.cloned.1.call-start = ((), (), s32[]{:S(2)}) async-start(), calls=%async_computation.6 | async-start | bytes 2097152 | tf_op jit(solution)/shard_map/psum | solution.py:111
  339.5 1.0 copy-start
  342.0 3.6 copy-start.1
  360.5 1.0 copy-start
  363.0 3.6 copy-start.1
  381.5 1.0 copy-start
  384.0 3.6 copy-start.1
  402.5 1.0 copy-start
  405.0 3.6 copy-start.1
Sparse Core Ops, SparseCore 0:
  195.9 20.4 all-reduce.2
  435.9 20.9 all-reduce.4
where the time goes:
time: 522 us; the launch traced here: 520 us
  waiting for transfers between devices  130 us (25%)
  blocking collectives  127 us (24%)
  local copies, waits for them, and re-layouts  85.6 us (16%)
  other arithmetic  49.9 us (10%)
  matrix products  47.2 us (9%)
  loops' own time  47.1 us (9%)
  starting transfers between devices  17.8 us (3%)
  between operations  15 us (3%)
    all_to_all x2, waiting for transfers between devices, per_device(): lax.all_to_all(outgoing, 'blk', split_axis=0, concat_axis=0, tiled=True)  88.2 us
    psum x2, blocking collectives, per_device(): gram = lax.psum(gram_of(mapped), 'blk') / total_rows  74.8 us
    all_to_all x2, blocking collectives, per_device(): lax.all_to_all(outbox, 'blk', split_axis=0, concat_axis=0, tiled=True)  52.5 us
    another operation x2, loops' own time, per_device(): lax.fori_loop(0, count, apply_pair, (sums_init, outbox_init, stored))  47.1 us
    psum x2, waiting for transfers between devices, per_device(): combined = lax.psum(sums, 'rep')  41.7 us
    scatter-add x16, local copies, waits for them, and re-layouts, apply_pair(): sums = sums.at[here].add(forward)  18.9 us
    dot_general x8, matrix products, gauss_tile(): lax.dot_general(left, right, (((1,), (1,)), ((), ())), preferred_element_...  16.3 us
    another operation x6, other arithmetic, per_device(): factor = jnp.linalg.cholesky(gram)  13 us
  transfers between devices with their start and end apart: 5, of which 4 were waited for; matrix products, arithmetic and copies ran while one was open for 1% of the time, Pallas kernels for 0%

commit v1 on v0

v1 whole, which is shorter than its diff:
```python
import functools

import jax
import jax.numpy as jnp
from jax import lax
from jax.experimental import pallas as pl
from jax.experimental.pallas import tpu as pltpu
from jax.sharding import PartitionSpec as P

BS = 1024
ITERS = 2
HALF = BS // 2
QTR = BS // 4
DEAD = 100000
MESH = pl.DeviceIdType.MESH
F32 = jnp.float32
BF16 = jnp.bfloat16
HI = lax.Precision.HIGHEST
NN = ((1,), (0,))
NT = ((1,), (1,))
TN = ((0,), (0,))


def mm(a, b, dims, precision=None):
    return lax.dot_general(
        a, b, (dims, ((), ())), precision=precision, preferred_element_type=F32
    )


def rows_cols(shape):
    return (
        lax.broadcasted_iota(jnp.int32, shape, 0),
        lax.broadcasted_iota(jnp.int32, shape, 1),
    )


def flags(cond, dtype=BF16):
    return jnp.where(cond, 1.0, 0.0).astype(dtype)


def cholesky_and_inverse(gram, n):
    rows, cols = rows_cols((n, 2 * n))
    a = jnp.where(cols < n, gram, flags(cols == rows + n, F32))
    row_id = lax.broadcasted_iota(jnp.int32, (n, 1), 0)
    for j in range(n - 1):
        col = jnp.sum(jnp.where(cols == j, a, 0.0), axis=1, keepdims=True)
        mult = jnp.where(row_id > j, col, 0.0) / col[j : j + 1, :]
        a = a - mult * a[j : j + 1, :]
    diag = jnp.sum(jnp.where(cols == rows, a, 0.0), axis=1, keepdims=True)
    return a * lax.rsqrt(diag)


def kernel(
    peers, blocks, width, slots, total_rows,
    frames, degree, start, block_slot, pairs, count,
    out, factor,
    info, table, fw, yw, scale, fsend, frecv, ysend, yrecv, fa, q, rhs, z, zs,
    bsend, brecv, eb, zx1, zx2, gx, chol,
    info_s, info_r, table_s, fs, fr, ys, yr, bs, br, zsem_s, zsem_r, gs, gr, yos, yor,
):
    me = lax.axis_index("blk")
    r = lax.axis_index("rep")
    k = 2 * me + r
    devs = 2 * peers
    per = peers // 2
    lanes = blocks * width

    def dev(kk):
        return {"blk": kk // 2, "rep": lax.rem(kk, 2)}

    barrier = pltpu.get_barrier_semaphore()

    def greet(t, _):
        pl.semaphore_signal(
            barrier, inc=1, device_id=dev(lax.rem(k + t, devs)), device_id_type=MESH
        )
        return 0

    lax.fori_loop(1, devs, greet, 0)

    lane = lax.broadcasted_iota(jnp.int32, (1, 128), 1)
    mine = jnp.zeros((1, 128), jnp.int32)
    live_count = count[0]
    for s in range(slots):
        mine = jnp.where(lane == s, block_slot[pairs[2 * s]], mine)
        mine = jnp.where(lane == 16 + s, block_slot[pairs[2 * s + 1]], mine)
        mine = jnp.where(lane == 32 + s, jnp.where(s < live_count, 1, 0), mine)
    info[k] = mine

    sel_r, sel_c = rows_cols((width, lanes))
    acc = jnp.zeros((BS, lanes), F32)
    for b in range(blocks):
        acc = acc + mm(frames[b * BS : (b + 1) * BS, :], flags(sel_c == sel_r + b * width), NN)
    fw[...] = acc.astype(BF16)

    pl.semaphore_wait(barrier, devs - 1)

    def info_copy(t, src):
        return pltpu.make_async_remote_copy(
            src_ref=info.at[src], dst_ref=info.at[src],
            send_sem=info_s.at[t], recv_sem=info_r.at[src],
            device_id=dev(lax.rem(k + t, devs)), device_id_type=MESH,
        )

    def info_send(t, _):
        info_copy(t, k).start()
        return 0

    lax.fori_loop(1, devs, info_send, 0)

    gr_r, gr_c = rows_cols((blocks, lanes))
    spread = flags(gr_c // width == gr_r, F32)
    scale[...] = lax.rsqrt(mm(degree[...], spread, TN, HI))
    acc = jnp.zeros((BS, lanes), F32)
    for b in range(blocks):
        acc = acc + mm(
            start[b * BS : (b + 1) * BS, :], flags(sel_c == sel_r + b * width, F32), NN, HI
        )
    yw[0] = (acc * scale[...]).astype(BF16)

    def info_wait(t, _):
        info_copy(t, lax.rem(k + t, devs)).wait_recv()
        return 0

    lax.fori_loop(1, devs, info_wait, 0)
    to_table = pltpu.make_async_copy(info, table, table_s)
    to_table.start()
    to_table.wait()

    def entries(owner):
        for half in range(2):
            for s in range(slots):
                row = table[2 * owner + half, 0, s]
                col = table[2 * owner + half, 0, 16 + s]
                alive = table[2 * owner + half, 0, 32 + s]
                yield row, col, alive

    def asked(d):
        low = me * blocks
        found = jnp.int32(-DEAD)
        for _, col, alive in entries(lax.rem(me + d, peers)):
            hit = (col >= low) & (col < low + blocks) & (alive == 1)
            found = found + jnp.where(hit, col - low + DEAD, 0)
        return found

    def own(d, skip_equal):
        low = lax.rem(me - d + peers, peers) * blocks
        found = jnp.int32(-DEAD)
        for row, col, alive in entries(me):
            hit = (col >= low) & (col < low + blocks) & (alive == 1)
            if skip_equal:
                hit = hit & (row != col)
            found = found + jnp.where(hit, row - me * blocks + DEAD, 0)
        return found

    pk_r, pk_c = rows_cols((lanes, 2 * width))

    def pack(source, it, first, block):
        top = pl.multiple_of(first, HALF)
        upper = source(pl.ds(top, QTR))
        lower = source(pl.ds(pl.multiple_of(top + QTR, QTR), QTR))
        want = pk_r - block * width
        got = mm(upper, flags((want == pk_c) & (pk_c < width)), NN)
        got = got + mm(lower, flags((want == pk_c - width) & (pk_c >= width)), NN)
        return got.astype(BF16)

    def block_copy(send, recv, ssem, rsem, d, half):
        return pltpu.make_async_remote_copy(
            src_ref=send.at[d], dst_ref=recv.at[d // 2, half],
            send_sem=ssem.at[d], recv_sem=rsem.at[d // 2, half],
            device_id={"blk": lax.rem(me + d, peers), "rep": lax.rem(d, 2)},
            device_id_type=MESH,
        )

    def send_blocks(source, it, send, recv, ssem, rsem):
        def one(d, _):
            send[d] = pack(source, it, r * HALF, asked(d))
            block_copy(send, recv, ssem, rsem, d, r).start()
            return 0

        lax.fori_loop(1, peers, one, 0)

    def fill_own(source, recv):
        @pl.when(r == 0)
        def _():
            block = asked(0)
            for half in range(2):
                recv[0, half] = pack(source, 0, half * HALF, block)

    def wait_blocks(m, send, recv, ssem, rsem):
        @pl.when(2 * m + r != 0)
        def _():
            for half in range(2):
                pltpu.make_async_remote_copy(
                    src_ref=send.at[0], dst_ref=recv.at[m, half],
                    send_sem=ssem.at[0], recv_sem=rsem.at[m, half],
                    device_id={"blk": me, "rep": 1 - r}, device_id_type=MESH,
                ).wait_recv()

    def from_fw(idx):
        return fw[idx, :]

    send_blocks(from_fw, 0, fsend, frecv, fs, fr)
    fill_own(from_fw, frecv)
    send_blocks(lambda idx: yw[0, idx, :], 0, ysend.at[0], yrecv.at[0], ys.at[0], yr.at[0])

    on_r, on_c = rows_cols((8, 2 * width))
    ones8 = flags(on_c // width == on_r, F32) * (1.0 / 16.0)

    def make_tile(m, _):
        block = own(2 * m + r, False)
        want = pk_r - block * width
        for u in range(2):
            pick = (want == pk_c - u * width) & (pk_c // width == u)
            fa[u] = (mm(fw[...], flags(pick), NN) * 0.125).astype(BF16)
        wait_blocks(m, fsend, frecv, fs, fr)
        right_sq = []
        for h in range(2):
            sq = jnp.square(frecv[m, h].astype(F32))
            right_sq.append(mm(ones8, sq, NT, HI))

        def chunk(p, _):
            at = pl.ds(pl.multiple_of(p * QTR, QTR), QTR)
            left_sq = jnp.sum(jnp.square(fa[0, at, :].astype(F32)), axis=1, keepdims=True) * 4.0
            for h in range(2):
                for u in range(2):
                    cross = mm(fa[u, at, :], frecv[m, h], NT)
                    dist = left_sq + right_sq[h][u : u + 1, :]
                    col = h * HALF + u * QTR
                    q[m, at, col : col + QTR] = jnp.exp(cross - dist).astype(BF16)
            return 0

        lax.fori_loop(0, 4, chunk, 0)
        return 0

    lax.fori_loop(0, per, make_tile, 0)

    rh_r, rh_c = rows_cols((2 * width, lanes))
    ba_r, ba_c = rows_cols((width, lanes))

    def back_copy(it, m):
        return pltpu.make_async_remote_copy(
            src_ref=bsend.at[it, m], dst_ref=brecv.at[it, m],
            send_sem=bs.at[it, m], recv_sem=br.at[it, m],
            device_id={"blk": lax.rem(me - 2 * m - r + peers, peers), "rep": r},
            device_id_type=MESH,
        )

    for it in range(ITERS):
        last = it == ITERS - 1
        fill_own(lambda idx: yw[it, idx, :], yrecv.at[it])
        z[...] = jnp.zeros((BS, lanes), F32)

        def product(m, _):
            d = 2 * m + r
            back_block = own(d, True)
            y_t = mm(flags(ba_c == ba_r + back_block * width), yw[it], NT).astype(BF16)
            bsend[it, m] = mm(y_t, q[m], NN).astype(BF16)

            @pl.when(d != 0)
            def _():
                back_copy(it, m).start()

            @pl.when(d == 0)
            def _():
                brecv[it, m] = bsend[it, m]

            block = own(d, False)
            wait_blocks(m, ysend.at[it], yrecv.at[it], ys.at[it], yr.at[it])
            for h in range(2):
                for u in range(2):
                    place = flags((rh_r - u * width == rh_c - block * width) & (rh_r // width == u))
                    at = h * HALF + u * QTR
                    rhs[at : at + QTR, :] = mm(yrecv[it, m, h], place, NN).astype(BF16)

            def chunk(p, _):
                at = pl.ds(pl.multiple_of(p * QTR, QTR), QTR)
                z[at, :] += mm(q[m, at, :], rhs[...], NN)
                return 0

            lax.fori_loop(0, 4, chunk, 0)
            return 0

        lax.fori_loop(0, per, product, 0)

        def collect(m, _):
            d = 2 * m + r
            eb[m] = flags(ba_c == ba_r + asked(d) * width)

            @pl.when(d != 0)
            def _():
                back_copy(it, m).wait_recv()

            return 0

        lax.fori_loop(0, per, collect, 0)
        z[...] += mm(
            brecv[it].reshape(per * width, BS), eb[...].reshape(per * width, lanes), TN
        )

        twin = {"blk": me, "rep": 1 - r}
        if last:
            zs[0] = z[:, : lanes // 2]
            zs[1] = z[:, lanes // 2 :]
            swap = pltpu.make_async_remote_copy(
                src_ref=zs.at[1 - r], dst_ref=zx2, send_sem=zsem_s.at[it],
                recv_sem=zsem_r.at[it], device_id=twin, device_id_type=MESH,
            )
        else:
            swap = pltpu.make_async_remote_copy(
                src_ref=z.at[pl.ds(pl.multiple_of((1 - r) * HALF, HALF), HALF), :],
                dst_ref=zx1, send_sem=zsem_s.at[it],
                recv_sem=zsem_r.at[it], device_id=twin, device_id_type=MESH,
            )
        swap.start()
        swap.wait()
        if last:
            first = jnp.where(r == 0, 1.0, 0.0)
            mine_scale = scale[:, : lanes // 2] * first + scale[:, lanes // 2 :] * (1.0 - first)
            w = (zs[r] + zx2[...]) * mine_scale
        else:
            rows = pl.ds(pl.multiple_of(r * HALF, HALF), HALF)
            mine_scale = scale[rows, :]
            w = (z[rows, :] + zx1[...]) * mine_scale
        wl = w.shape[1]

        gg = mm(w, w, TN, HI)
        g_r, g_c = rows_cols((wl, wl))
        gg = jnp.where(g_r // width == g_c // width, gg, 0.0)
        a_r, a_c = rows_cols((width, wl))
        fold = flags(a_c % width == a_r, F32)
        b_r, b_c = rows_cols((2 * width, wl))
        fold_wide = flags(b_c % width == b_r, F32)
        gx[it, k] = mm(mm(fold, gg, NN, HI), fold_wide, NT, HI)

        def gram_copy(t, src):
            return pltpu.make_async_remote_copy(
                src_ref=gx.at[it, src], dst_ref=gx.at[it, src],
                send_sem=gs.at[it, t], recv_sem=gr.at[it, src],
                device_id=dev(lax.rem(k + t, devs)), device_id_type=MESH,
            )

        def gram_send(t, _):
            gram_copy(t, k).start()
            return 0

        def gram_wait(t, _):
            gram_copy(t, lax.rem(k + t, devs)).wait_recv()
            return 0

        def gram_done(t, _):
            gram_copy(t, k).wait_send()
            return 0

        lax.fori_loop(1, devs, gram_send, 0)
        lax.fori_loop(1, devs, gram_wait, 0)
        gram = gx[it, 0]
        for t in range(1, devs):
            gram = gram + gx[it, t]
        chol[...] = cholesky_and_inverse(gram * (1.0 / total_rows), width)

        c_r, c_c = rows_cols((wl, 2 * width))
        inv_t = mm(flags(c_c == width + c_r % width, F32), chol[...], NT, HI)
        t_r, t_c = rows_cols((width, wl))
        tiled = mm(inv_t, flags(t_c % width == t_r, F32), NN, HI)
        v = mm(w, jnp.where(g_r // width == g_c // width, tiled, 0.0), NN, HI)
        if last:
            for b in range(blocks // 2):
                p_r, p_c = rows_cols((wl, width))
                out[b * BS : (b + 1) * BS, :] = v[:, b * width : (b + 1) * width]
            l_r, l_c = rows_cols((width, 2 * width))
            factor[...] = mm(flags(l_r == l_c, F32), chol[...], NT, HI)
        else:
            yw[it + 1, rows, :] = (v * mine_scale).astype(BF16)
            give = pltpu.make_async_remote_copy(
                src_ref=yw.at[it + 1, rows, :], dst_ref=yw.at[it + 1, rows, :],
                send_sem=yos, recv_sem=yor, device_id=twin, device_id_type=MESH,
            )
            give.start()
            nxt = it + 1
            send_blocks(
                lambda idx: yw[nxt, idx, :], nxt,
                ysend.at[nxt], yrecv.at[nxt], ys.at[nxt], yr.at[nxt],
            )
            other = pl.ds(pl.multiple_of((1 - r) * HALF, HALF), HALF)
            give.wait_send()
            pltpu.make_async_remote_copy(
                src_ref=yw.at[it + 1, other, :], dst_ref=yw.at[it + 1, other, :],
                send_sem=yos, recv_sem=yor, device_id=twin, device_id_type=MESH,
            ).wait_recv()
        lax.fori_loop(1, devs, gram_done, 0)

    def blocks_done(d, _):
        block_copy(fsend, frecv, fs, fr, d, r).wait_send()
        for it in range(ITERS):
            block_copy(ysend.at[it], yrecv.at[it], ys.at[it], yr.at[it], d, r).wait_send()
        return 0

    lax.fori_loop(1, peers, blocks_done, 0)

    def info_done(t, _):
        info_copy(t, k).wait_send()
        return 0

    lax.fori_loop(1, devs, info_done, 0)

    def back_done(m, _):
        @pl.when(2 * m + r != 0)
        def _():
            for it in range(ITERS):
                back_copy(it, m).wait_send()

        return 0

    lax.fori_loop(0, per, back_done, 0)


def per_device(frames, degree, start, block_slot, pair_list, pair_count):
    peers = lax.axis_size("blk")
    local_rows, width = start.shape
    blocks = local_rows // BS
    slots = pair_list.shape[2]
    per = peers // 2
    devs = 2 * peers
    lanes = blocks * width
    dma = pltpu.SemaphoreType.DMA
    vmem = pl.BlockSpec(memory_space=pltpu.VMEM)
    smem = pl.BlockSpec(memory_space=pltpu.SMEM)
    scratch = [
        pltpu.VMEM((devs, 1, 128), jnp.int32),
        pltpu.SMEM((devs, 1, 128), jnp.int32),
        pltpu.VMEM((BS, lanes), BF16),
        pltpu.VMEM((ITERS, BS, lanes), BF16),
        pltpu.VMEM((BS, lanes), F32),
        pltpu.VMEM((peers, QTR, 2 * width), BF16),
        pltpu.VMEM((per, 2, QTR, 2 * width), BF16),
        pltpu.VMEM((ITERS, peers, QTR, 2 * width), BF16),
        pltpu.VMEM((ITERS, per, 2, QTR, 2 * width), BF16),
        pltpu.VMEM((2, BS, 2 * width), BF16),
        pltpu.VMEM((per, BS, BS), BF16),
        pltpu.VMEM((BS, lanes), BF16),
        pltpu.VMEM((BS, lanes), F32),
        pltpu.VMEM((2, BS, lanes // 2), F32),
        pltpu.VMEM((ITERS, per, width, BS), BF16),
        pltpu.VMEM((ITERS, per, width, BS), BF16),
        pltpu.VMEM((per, width, lanes), BF16),
        pltpu.VMEM((HALF, lanes), F32),
        pltpu.VMEM((BS, lanes // 2), F32),
        pltpu.VMEM((ITERS, devs, width, 2 * width), F32),
        pltpu.VMEM((width, 2 * width), F32),
        dma((devs,)), dma((devs,)), dma,
        dma((peers,)), dma((per, 2)),
        dma((ITERS, peers)), dma((ITERS, per, 2)),
        dma((ITERS, per)), dma((ITERS, per)),
        dma((ITERS,)), dma((ITERS,)),
        dma((ITERS, devs)), dma((ITERS, devs)),
        dma, dma,
    ]
    return pl.pallas_call(
        functools.partial(kernel, peers, blocks, width, slots, local_rows * peers),
        out_shape=(
            jax.ShapeDtypeStruct((local_rows // 2, width), F32),
            jax.ShapeDtypeStruct((width, width), F32),
        ),
        in_specs=[vmem, vmem, vmem, smem, smem, smem],
        out_specs=(vmem, vmem),
        scratch_shapes=scratch,
        compiler_params=pltpu.CompilerParams(
            collective_id=0, has_side_effects=True, vmem_limit_bytes=56 * 1024 * 1024
        ),
    )(
        frames,
        degree.reshape(blocks, BS),
        start,
        block_slot,
        pair_list.reshape(-1),
        pair_count.reshape(-1),
    )


def solution(mesh):
    placed = (
        P(("groups", "blk"), None),
        P(("groups", "blk")),
        P(("groups", "blk"), None),
        P("groups"),
        P(("groups", "blk"), "rep", None, None),
        P(("groups", "blk"), "rep"),
    )
    return jax.shard_map(
        per_device,
        mesh=mesh,
        in_specs=placed,
        out_specs=(P(("groups", "blk", "rep"), None), P("groups", None)),
        check_vma=False,
    )
```

time: 522 us -> 134 us (0.26)
  the two profiles are of different devices: /device:TPU:0 before, /device:TPU:11 now
where the time goes in v1:
time: 134 us
  Pallas kernels  122 us (91%)
  local copies, waits for them, and re-layouts  10.7 us (8%)
  between operations  1.38 us (1%)
    pallas_call x1, Pallas kernels, per_device(): pl.pallas_call(functools.partial(kernel, peers, blocks, width, slots, loc...  122 us
    unnamed x6, local copies, waits for them, and re-layouts  6.47 us

profile of v1, /device:TPU:11, one launch (start us, length us, event | category | flops | bytes accessed | tf_op | source)
XLA Modules:
  0.0 134.1 jit_solution(9695585359086830207)
XLA Ops:
  0.6 0.0 copy-start
  1.4 0.8 copy.12
  2.1 0.6 reshape.14.pairs
  2.7 1.3 reshape.13.degree
  4.1 2.4 %copy.13.frames = bf16[4096,64]{1,0:T(8,128)(2,1)} copy(bf16[4096,64]{0,1:T(8,128)(2,1)} %param.6) | data formatting | bytes 1048576 | tf_op args[0]
  6.4 0.0 copy-done
  6.4 2.0 %copy.14.start = f32[4096,64]{1,0:T(8,128)} copy(f32[4096,64]{0,1:T(8,128)S(1)} %copy-done) | data formatting | bytes 2097152 | tf_op args[2]
  8.4 122.0 %shard_map.77 = (f32[2048,64]{1,0:T(8,128)}, f32[64,64]{1,0:T(8,128)}) custom-call(bf16[4096,64]{1,0:T(8,128)(2,1)} %copy.13.frames, f32[4,1024]{1,0:T(4,128)} %reshape.13.degree, f32[4096,64]{1,0:T(8,128)} %copy.14.start, s32[32]{0:T(128)} %block_slot.1, s32[8]{0:T(128)} %reshape.14.pairs, s32[1]{0:T(128)} %bitcast.1.count), custom_call_target="tpu_custom_call" | custom-call | tf_op jit(solution)/shard_map/pallas_call | solution.py:459
  130.4 2.3 %copy.15 = f32[2048,64]{0,1:T(8,128)} copy(f32[2048,64]{1,0:T(8,128)} %get-tuple-element.4) | data formatting | bytes 1048576 | tf_op jit(solution)/shard_map/pallas_call | solution.py:459
  132.7 1.4 %copy.18 = f32[64,64]{1,0:T(8,128)} copy(f32[64,64]{1,0:T(8,128)} %get-tuple-element.9) | data formatting | bytes 32768
Async XLA Ops:
  0.6 5.8 %copy-start = (f32[4096,64]{0,1:T(8,128)S(1)}, f32[4096,64]{0,1:T(8,128)}, u32[]{:S(2)}) copy-start(f32[4096,64]{0,1:T(8,128)} %param.8) | copy-start | bytes 3145732

commit v2 on v1

v2 whole, which is shorter than its diff:
```python
import functools

import jax
import jax.numpy as jnp
from jax import lax
from jax.experimental import pallas as pl
from jax.experimental.pallas import tpu as pltpu
from jax.sharding import PartitionSpec as P

BS = 1024
ITERS = 2
HALF = BS // 2
CHUNK = BS // 4
MESH = pl.DeviceIdType.MESH
F32 = jnp.float32
BF16 = jnp.bfloat16
HI = lax.Precision.HIGHEST
NN = ((1,), (0,))
NT = ((1,), (1,))
TN = ((0,), (0,))


def mm(a, b, dims, precision=None):
    return lax.dot_general(
        a, b, (dims, ((), ())), precision=precision, preferred_element_type=F32
    )


def rows_cols(shape):
    return (
        lax.broadcasted_iota(jnp.int32, shape, 0),
        lax.broadcasted_iota(jnp.int32, shape, 1),
    )


def flags(cond, dtype=BF16):
    return jnp.where(cond, 1.0, 0.0).astype(dtype)


def cholesky_and_inverse(gram, n):
    rows, cols = rows_cols((n, 2 * n))
    a = jnp.where(cols < n, gram, flags(cols == rows + n, F32))
    row_id = lax.broadcasted_iota(jnp.int32, (n, 1), 0)
    for j in range(n - 1):
        col = jnp.sum(jnp.where(cols == j, a, 0.0), axis=1, keepdims=True)
        mult = jnp.where(row_id > j, col, 0.0) / col[j : j + 1, :]
        a = a - mult * a[j : j + 1, :]
    diag = jnp.sum(jnp.where(cols == rows, a, 0.0), axis=1, keepdims=True)
    return a * lax.rsqrt(diag)


def kernel(
    peers, blocks, width, slots, total_rows,
    frames, degree, start, block_slot, pairs, count,
    out, factor,
    info, table, ft, fn, yt, scale, fsend, frecv, ysend, yrecv, q, ypl, zt, zx,
    bsend, brecv, eb, gx, chol,
    info_s, info_r, table_s, fs, fr, ys, yr, bs, br, zsem_s, zsem_r, gs, gr,
):
    me = lax.axis_index("blk")
    r = lax.axis_index("rep")
    k = 2 * me + r
    devs = 2 * peers
    per = peers // 2
    half_w = width // 2
    twin = {"blk": me, "rep": 1 - r}

    def dev(kk):
        return {"blk": kk // 2, "rep": lax.rem(kk, 2)}

    barrier = pltpu.get_barrier_semaphore()

    def greet(t, _):
        pl.semaphore_signal(
            barrier, inc=1, device_id=dev(lax.rem(k + t, devs)), device_id_type=MESH
        )
        return 0

    lax.fori_loop(1, devs, greet, 0)

    lane = lax.broadcasted_iota(jnp.int32, (1, 128), 1)
    mine = jnp.zeros((1, 128), jnp.int32)
    live_count = count[0]
    for s in range(slots):
        row = block_slot[pairs[2 * s]]
        col = block_slot[pairs[2 * s + 1]]
        peer = lax.div(col, blocks)
        alive = jnp.where(s < live_count, 1, 0)
        mine = jnp.where(lane == peer, (col - peer * blocks + 1) * alive, mine)
        mine = jnp.where(lane == 32 + peer, (row - me * blocks + 1) * alive, mine)
        mine = jnp.where(lane == 64 + peer, jnp.where(row != col, 1, 0) * alive, mine)
    info[k] = mine

    for b in range(blocks):
        at = slice(b * BS, (b + 1) * BS)
        ft[b] = frames[:, at]

    pl.semaphore_wait(barrier, devs - 1)

    def info_copy(t, src):
        return pltpu.make_async_remote_copy(
            src_ref=info.at[src], dst_ref=info.at[src],
            send_sem=info_s.at[t], recv_sem=info_r.at[src],
            device_id=dev(lax.rem(k + t, devs)), device_id_type=MESH,
        )

    def info_send(t, _):
        info_copy(t, k).start()
        return 0

    lax.fori_loop(1, devs, info_send, 0)

    for b in range(blocks):
        at = slice(b * BS, (b + 1) * BS)
        s_row = lax.rsqrt(degree[:, at])
        scale[b] = s_row
        yt[0, b] = (start[:, at] * s_row).astype(BF16)
        e_r, e_c = rows_cols((width, width))
        fn[b] = (mm(ft[b], flags(e_r == e_c), TN) * 0.125).astype(BF16)

    def info_wait(t, _):
        info_copy(t, lax.rem(k + t, devs)).wait_recv()
        return 0

    lax.fori_loop(1, devs, info_wait, 0)
    to_table = pltpu.make_async_copy(info, table, table_s)
    to_table.start()
    to_table.wait()

    def asked(d):
        owner = lax.rem(me + d, peers)
        return table[2 * owner, 0, me] + table[2 * owner + 1, 0, me] - 1

    def own(d):
        peer = 32 + lax.rem(me - d + peers, peers)
        return table[2 * me, 0, peer] + table[2 * me + 1, 0, peer] - 1

    def differ(d):
        peer = 64 + lax.rem(me - d + peers, peers)
        return table[2 * me, 0, peer] + table[2 * me + 1, 0, peer]

    def lanes_of(half):
        return pl.ds(pl.multiple_of(half * HALF, HALF), HALF)

    def block_copy(send, recv, ssem, rsem, d, half):
        return pltpu.make_async_remote_copy(
            src_ref=send.at[d], dst_ref=recv.at[d // 2, half],
            send_sem=ssem.at[d], recv_sem=rsem.at[d // 2, half],
            device_id={"blk": lax.rem(me + d, peers), "rep": lax.rem(d, 2)},
            device_id_type=MESH,
        )

    def send_blocks(source, send, recv, ssem, rsem):
        def one(d, _):
            send[d] = source[jnp.maximum(asked(d), 0), :, lanes_of(r)]
            block_copy(send, recv, ssem, rsem, d, r).start()
            return 0

        lax.fori_loop(1, peers, one, 0)

    def fill_own(source, recv):
        @pl.when(r == 0)
        def _():
            block = jnp.maximum(asked(0), 0)
            for half in range(2):
                recv[0, half] = source[block, :, half * HALF : (half + 1) * HALF]

    def wait_blocks(m, send, recv, ssem, rsem):
        @pl.when(2 * m + r != 0)
        def _():
            for half in range(2):
                pltpu.make_async_remote_copy(
                    src_ref=send.at[0], dst_ref=recv.at[m, half],
                    send_sem=ssem.at[0], recv_sem=rsem.at[m, half],
                    device_id=twin, device_id_type=MESH,
                ).wait_recv()

    send_blocks(ft, fsend, frecv, fs, fr)
    send_blocks(yt.at[0], ysend.at[0], yrecv.at[0], ys.at[0], yr.at[0])
    fill_own(ft, frecv)

    def back_copy(it, m):
        return pltpu.make_async_remote_copy(
            src_ref=bsend.at[it, m], dst_ref=brecv.at[it, m],
            send_sem=bs.at[it, m], recv_sem=br.at[it, m],
            device_id={"blk": lax.rem(me - 2 * m - r + peers, peers), "rep": r},
            device_id_type=MESH,
        )

    def send_back(it, m):
        d = 2 * m + r
        keep = jnp.where(differ(d) > 0, 1.0, 0.0)
        y_a = (yt[it, jnp.maximum(own(d), 0)].astype(F32) * keep).astype(BF16)
        bsend[it, m] = mm(y_a, q[m], NN).astype(BF16)

        @pl.when(d != 0)
        def _():
            back_copy(it, m).start()

        @pl.when(d == 0)
        def _():
            brecv[it, m] = bsend[it, m]

    def make_tile(m, _):
        block = jnp.maximum(own(2 * m + r), 0)
        wait_blocks(m, fsend, frecv, fs, fr)
        right_sq = [
            jnp.sum(jnp.square(frecv[m, h].astype(F32)), axis=0, keepdims=True) * (1.0 / 16.0)
            for h in range(2)
        ]

        def chunk(p, _):
            at = pl.ds(pl.multiple_of(p * CHUNK, CHUNK), CHUNK)
            left = fn[block, at, :]
            left_sq = jnp.sum(jnp.square(left.astype(F32)), axis=1, keepdims=True) * 4.0
            for h in range(2):
                cross = mm(left, frecv[m, h], NN)
                dist = left_sq + right_sq[h]
                q[m, at, h * HALF : (h + 1) * HALF] = jnp.exp(cross - dist).astype(BF16)
            return 0

        lax.fori_loop(0, BS // CHUNK, chunk, 0)
        send_back(0, m)
        return 0

    lax.fori_loop(0, per, make_tile, 0)

    pl_r, pl_c = rows_cols((blocks * width, width))

    for it in range(ITERS):
        last = it == ITERS - 1
        fill_own(yt.at[it], yrecv.at[it])
        if it > 0:

            def back(m, _):
                send_back(it, m)
                return 0

            lax.fori_loop(0, per, back, 0)
        zt[...] = jnp.zeros_like(zt)

        def product(m, _):
            wait_blocks(m, ysend.at[it], yrecv.at[it], ys.at[it], yr.at[it])
            place = flags(pl_r == pl_c + own(2 * m + r) * width)
            for h in range(2):
                ypl[:, h * HALF : (h + 1) * HALF] = mm(place, yrecv[it, m, h], NN).astype(BF16)

            def chunk(p, _):
                at = pl.ds(pl.multiple_of(p * CHUNK, CHUNK), CHUNK)
                zt[:, at] += mm(ypl[...], q[m, at, :], NT)
                return 0

            lax.fori_loop(0, BS // CHUNK, chunk, 0)
            return 0

        lax.fori_loop(0, per, product, 0)

        def collect(m, _):
            d = 2 * m + r
            eb[m] = flags((pl_r == pl_c + asked(d) * width) & (asked(d) >= 0))

            @pl.when(d != 0)
            def _():
                back_copy(it, m).wait_recv()

            return 0

        lax.fori_loop(0, per, collect, 0)
        total = zt[...]
        for m in range(per):
            total = total + mm(eb[m], brecv[it, m], NN)
        zt[...] = total

        swap = pltpu.make_async_remote_copy(
            src_ref=zt, dst_ref=zx.at[it], send_sem=zsem_s.at[it],
            recv_sem=zsem_r.at[it], device_id=twin, device_id_type=MESH,
        )
        swap.start()
        swap.wait()
        for b in range(blocks):
            at = slice(b * width, (b + 1) * width)
            zt[at, :] = (zt[at, :] + zx[it, at, :]) * scale[b]

        gram = jnp.zeros((2 * width, 2 * width), F32)
        for b in range(0, blocks, 2):
            w_t = zt[b * width : (b + 2) * width, :]
            gram = gram + mm(w_t, w_t, NT, HI)
        gram = gram[:width] + pltpu.roll(gram[width:], width, 1)
        low = rows_cols((half_w, 2 * width))[1] < width
        gx[it, me] = jnp.where(low, gram[:half_w], pltpu.roll(gram[half_w:], width, 1))

        def gram_copy(t, src):
            return pltpu.make_async_remote_copy(
                src_ref=gx.at[it, src], dst_ref=gx.at[it, src],
                send_sem=gs.at[it, t], recv_sem=gr.at[it, src],
                device_id={"blk": lax.rem(me + t, peers), "rep": r}, device_id_type=MESH,
            )

        def gram_send(t, _):
            gram_copy(t, me).start()
            return 0

        def gram_wait(t, _):
            gram_copy(t, lax.rem(me + t, peers)).wait_recv()
            return 0

        def gram_done(t, _):
            gram_copy(t, me).wait_send()
            return 0

        lax.fori_loop(1, peers, gram_send, 0)
        lax.fori_loop(1, peers, gram_wait, 0)
        gram = gx[it, 0]
        for t in range(1, peers):
            gram = gram + gx[it, t]
        gram = jnp.concatenate([gram, pltpu.roll(gram, width, 1)], axis=0)
        result = cholesky_and_inverse(gram * (1.0 / total_rows), width)

        inverse = pltpu.roll(result, width, 1)[:, :width]
        if last:
            for b in range(blocks // 2):
                at = pl.ds(pl.multiple_of((r * (blocks // 2) + b) * width, width), width)
                out[:, b * BS : (b + 1) * BS] = mm(inverse, zt[at, :], NN, HI)
            chol[...] = result
            l_r, l_c = rows_cols((width, 2 * width))
            factor[...] = mm(flags(l_r == l_c, F32), chol[...], NT, HI)
        else:
            for b in range(blocks):
                v_t = mm(inverse, zt[b * width : (b + 1) * width, :], NN, HI)
                yt[it + 1, b] = (v_t * scale[b]).astype(BF16)
            nxt = it + 1
            send_blocks(yt.at[nxt], ysend.at[nxt], yrecv.at[nxt], ys.at[nxt], yr.at[nxt])
        lax.fori_loop(1, peers, gram_done, 0)

    def blocks_done(d, _):
        block_copy(fsend, frecv, fs, fr, d, r).wait_send()
        for it in range(ITERS):
            block_copy(ysend.at[it], yrecv.at[it], ys.at[it], yr.at[it], d, r).wait_send()
        return 0

    lax.fori_loop(1, peers, blocks_done, 0)

    def info_done(t, _):
        info_copy(t, k).wait_send()
        return 0

    lax.fori_loop(1, devs, info_done, 0)

    def back_done(m, _):
        @pl.when(2 * m + r != 0)
        def _():
            for it in range(ITERS):
                back_copy(it, m).wait_send()

        return 0

    lax.fori_loop(0, per, back_done, 0)


def per_device(frames, degree, start, block_slot, pair_list, pair_count):
    peers = lax.axis_size("blk")
    local_rows, width = start.shape
    blocks = local_rows // BS
    slots = pair_list.shape[2]
    per = peers // 2
    devs = 2 * peers
    dma = pltpu.SemaphoreType.DMA
    vmem = pl.BlockSpec(memory_space=pltpu.VMEM)
    smem = pl.BlockSpec(memory_space=pltpu.SMEM)
    scratch = [
        pltpu.VMEM((devs, 1, 128), jnp.int32),
        pltpu.SMEM((devs, 1, 128), jnp.int32),
        pltpu.VMEM((blocks, width, BS), BF16),
        pltpu.VMEM((blocks, BS, width), BF16),
        pltpu.VMEM((ITERS, blocks, width, BS), BF16),
        pltpu.VMEM((blocks, 1, BS), F32),
        pltpu.VMEM((peers, width, HALF), BF16),
        pltpu.VMEM((per, 2, width, HALF), BF16),
        pltpu.VMEM((ITERS, peers, width, HALF), BF16),
        pltpu.VMEM((ITERS, per, 2, width, HALF), BF16),
        pltpu.VMEM((per, BS, BS), BF16),
        pltpu.VMEM((blocks * width, BS), BF16),
        pltpu.VMEM((blocks * width, BS), F32),
        pltpu.VMEM((ITERS, blocks * width, BS), F32),
        pltpu.VMEM((ITERS, per, width, BS), BF16),
        pltpu.VMEM((ITERS, per, width, BS), BF16),
        pltpu.VMEM((per, blocks * width, width), BF16),
        pltpu.VMEM((ITERS, peers, width // 2, 2 * width), F32),
        pltpu.VMEM((width, 2 * width), F32),
        dma((devs,)), dma((devs,)), dma,
        dma((peers,)), dma((per, 2)),
        dma((ITERS, peers)), dma((ITERS, per, 2)),
        dma((ITERS, per)), dma((ITERS, per)),
        dma((ITERS,)), dma((ITERS,)),
        dma((ITERS, peers)), dma((ITERS, peers)),
    ]
    out_t, factor = pl.pallas_call(
        functools.partial(kernel, peers, blocks, width, slots, local_rows * peers),
        out_shape=(
            jax.ShapeDtypeStruct((width, local_rows // 2), F32),
            jax.ShapeDtypeStruct((width, width), F32),
        ),
        in_specs=[vmem, vmem, vmem, smem, smem, smem],
        out_specs=(vmem, vmem),
        scratch_shapes=scratch,
        compiler_params=pltpu.CompilerParams(
            collective_id=0, has_side_effects=True, vmem_limit_bytes=56 * 1024 * 1024
        ),
    )(
        frames.T,
        degree.reshape(1, local_rows),
        start.T,
        block_slot,
        pair_list.reshape(-1),
        pair_count.reshape(-1),
    )
    return out_t.T, factor


def solution(mesh):
    placed = (
        P(("groups", "blk"), None),
        P(("groups", "blk")),
        P(("groups", "blk"), None),
        P("groups"),
        P(("groups", "blk"), "rep", None, None),
        P(("groups", "blk"), "rep"),
    )
    return jax.shard_map(
        per_device,
        mesh=mesh,
        in_specs=placed,
        out_specs=(P(("groups", "blk", "rep"), None), P("groups", None)),
        check_vma=False,
    )
```

time: 134 us -> 113 us (0.84)
  the two profiles are of different devices: /device:TPU:11 before, /device:TPU:0 now
where the time goes in v2:
time: 113 us; the launch traced here: 112 us
  Pallas kernels  107 us (95%)
  local copies, waits for them, and re-layouts  3.86 us (3%)
  between operations  1.3 us (1%)
    pallas_call x1, Pallas kernels, per_device(): pl.pallas_call(functools.partial(kernel, peers, blocks, width, slots, loc...  107 us
    unnamed x7, local copies, waits for them, and re-layouts  3.26 us

profile of v2, /device:TPU:0, one launch (start us, length us, event | category | flops | bytes accessed | tf_op | source)
XLA Modules:
  0.0 112.5 jit_solution(14202478662689164771)
XLA Ops:
  1.3 0.0 copy-start.1
  1.3 0.7 copy-done.1
  2.0 0.1 copy.9
  2.0 0.6 reshape.14.pairs
  2.6 107.3 %shard_map.77 = (f32[64,2048]{1,0:T(8,128)}, f32[64,64]{1,0:T(8,128)}) custom-call(bf16[64,4096]{1,0:T(8,128)(2,1)} %bitcast.7, f32[1,4096]{1,0:T(1,128)} %bitcast.9, f32[64,4096]{1,0:T(8,128)} %bitcast.6, s32[32]{0:T(128)} %block_slot.1, s32[8]{0:T(128)} %reshape.14.pairs, s32[1]{0:T(128)} %bitcast.5.count), custom_call_target="tpu_custom_call" | custom-call | tf_op jit(solution)/shard_map/pallas_call | solution.py:397
  110.0 0.0 copy-start
  110.0 1.9 %copy.13 = f32[2048,64]{0,1:T(8,128)} copy(f32[2048,64]{0,1:T(8,128)} %bitcast.8) | data formatting | bytes 1048576
  111.9 0.0 copy-done
  111.9 0.6 copy.14
Async XLA Ops:
  1.3 0.7 copy-start.1
  110.0 1.9 %copy-start = (f32[64,64]{1,0:T(8,128)S(1)}, f32[64,64]{1,0:T(8,128)}, u32[]{:S(2)}) copy-start(f32[64,64]{1,0:T(8,128)} %get-tuple-element.9) | copy-start | bytes 49156

commit v3 on v2

--- a/solution.py
+++ b/solution.py
@@ -43,8 +43,9 @@
     row_id = lax.broadcasted_iota(jnp.int32, (n, 1), 0)
     for j in range(n - 1):
         col = jnp.sum(jnp.where(cols == j, a, 0.0), axis=1, keepdims=True)
-        mult = jnp.where(row_id > j, col, 0.0) / col[j : j + 1, :]
-        a = a - mult * a[j : j + 1, :]
+        pivot = a[j : j + 1, :]
+        inv = 1.0 / jnp.sum(jnp.where(cols[:1] == j, pivot, 0.0), axis=1, keepdims=True)
+        a = a - jnp.where(row_id > j, col, 0.0) * (pivot * inv)
     diag = jnp.sum(jnp.where(cols == rows, a, 0.0), axis=1, keepdims=True)
     return a * lax.rsqrt(diag)
 

time: 113 us -> 113 us (level)
  no operation moved by 1% of the time
where the time goes in v3:
time: 113 us
  Pallas kernels  108 us (96%)
  local copies, waits for them, and re-layouts  3.86 us (3%)
  between operations  1.3 us (1%)
    pallas_call x1, Pallas kernels, per_device(): pl.pallas_call(functools.partial(kernel, peers, blocks, width, slots, loc...  108 us
    unnamed x7, local copies, waits for them, and re-layouts  3.26 us

profile of v3, /device:TPU:0, one launch (start us, length us, event | category | flops | bytes accessed | tf_op | source)
XLA Modules:
  0.0 112.7 jit_solution(7731280221150411818)
XLA Ops:
  1.3 0.0 copy-start.1
  1.3 0.7 copy-done.1
  2.0 0.1 copy.9
  2.0 0.6 reshape.14.pairs
  2.6 107.5 %shard_map.77 = (f32[64,2048]{1,0:T(8,128)}, f32[64,64]{1,0:T(8,128)}) custom-call(bf16[64,4096]{1,0:T(8,128)(2,1)} %bitcast.7, f32[1,4096]{1,0:T(1,128)} %bitcast.9, f32[64,4096]{1,0:T(8,128)} %bitcast.6, s32[32]{0:T(128)} %block_slot.1, s32[8]{0:T(128)} %reshape.14.pairs, s32[1]{0:T(128)} %bitcast.5.count), custom_call_target="tpu_custom_call" | custom-call | tf_op jit(solution)/shard_map/pallas_call | solution.py:398
  110.2 0.0 copy-start
  110.2 1.9 %copy.13 = f32[2048,64]{0,1:T(8,128)} copy(f32[2048,64]{0,1:T(8,128)} %bitcast.8) | data formatting | bytes 1048576
  112.1 0.0 copy-done
  112.1 0.6 copy.14
Async XLA Ops:
  1.3 0.7 copy-start.1
  110.2 1.9 %copy-start = (f32[64,64]{1,0:T(8,128)S(1)}, f32[64,64]{1,0:T(8,128)}, u32[]{:S(2)}) copy-start(f32[64,64]{1,0:T(8,128)} %get-tuple-element.9) | copy-start | bytes 49156

commit v4 on v2

--- a/solution.py
+++ b/solution.py
@@ -266,19 +266,23 @@
             return 0
 
         lax.fori_loop(0, per, collect, 0)
-        total = zt[...]
-        for m in range(per):
-            total = total + mm(eb[m], brecv[it, m], NN)
-        zt[...] = total
-
-        swap = pltpu.make_async_remote_copy(
-            src_ref=zt, dst_ref=zx.at[it], send_sem=zsem_s.at[it],
-            recv_sem=zsem_r.at[it], device_id=twin, device_id_type=MESH,
-        )
-        swap.start()
-        swap.wait()
+        def swap(b):
+            at = slice(b * width, (b + 1) * width)
+            return pltpu.make_async_remote_copy(
+                src_ref=zt.at[at, :], dst_ref=zx.at[it, at, :], send_sem=zsem_s.at[it, b],
+                recv_sem=zsem_r.at[it, b], device_id=twin, device_id_type=MESH,
+            )
+
         for b in range(blocks):
             at = slice(b * width, (b + 1) * width)
+            total = zt[at, :]
+            for m in range(per):
+                total = total + mm(eb[m, at, :], brecv[it, m], NN)
+            zt[at, :] = total
+            swap(b).start()
+        for b in range(blocks):
+            at = slice(b * width, (b + 1) * width)
+            swap(b).wait()
             zt[at, :] = (zt[at, :] + zx[it, at, :]) * scale[b]
 
         gram = jnp.zeros((2 * width, 2 * width), F32)
@@ -391,7 +395,7 @@
         dma((peers,)), dma((per, 2)),
         dma((ITERS, peers)), dma((ITERS, per, 2)),
         dma((ITERS, per)), dma((ITERS, per)),
-        dma((ITERS,)), dma((ITERS,)),
+        dma((ITERS, blocks)), dma((ITERS, blocks)),
         dma((ITERS, peers)), dma((ITERS, peers)),
     ]
     out_t, factor = pl.pallas_call(

time: 113 us -> 111 us (0.982)
    pallas_call x1, Pallas kernels: 107 us -> 106 us  [per_device(): pl.pallas_call(functools.partial(kernel, peers, blocks, width, slots, loc...]
where the time goes in v4:
time: 111 us
  Pallas kernels  106 us (95%)
  local copies, waits for them, and re-layouts  3.86 us (3%)
  between operations  1.3 us (1%)
    pallas_call x1, Pallas kernels, per_device(): pl.pallas_call(functools.partial(kernel, peers, blocks, width, slots, loc...  106 us
    unnamed x7, local copies, waits for them, and re-layouts  3.26 us

profile of v4, /device:TPU:0, one launch (start us, length us, event | category | flops | bytes accessed | tf_op | source)
XLA Modules:
  0.0 111.1 jit_solution(5659676898318743743)
XLA Ops:
  1.3 0.0 copy-start.1
  1.3 0.7 copy-done.1
  2.0 0.1 copy.9
  2.0 0.6 reshape.14.pairs
  2.6 106.0 %shard_map.77 = (f32[64,2048]{1,0:T(8,128)}, f32[64,64]{1,0:T(8,128)}) custom-call(bf16[64,4096]{1,0:T(8,128)(2,1)} %bitcast.7, f32[1,4096]{1,0:T(1,128)} %bitcast.9, f32[64,4096]{1,0:T(8,128)} %bitcast.6, s32[32]{0:T(128)} %block_slot.1, s32[8]{0:T(128)} %reshape.14.pairs, s32[1]{0:T(128)} %bitcast.5.count), custom_call_target="tpu_custom_call" | custom-call | tf_op jit(solution)/shard_map/pallas_call | solution.py:401
  108.6 0.0 copy-start
  108.6 1.9 %copy.13 = f32[2048,64]{0,1:T(8,128)} copy(f32[2048,64]{0,1:T(8,128)} %bitcast.8) | data formatting | bytes 1048576
  110.5 0.0 copy-done
  110.5 0.6 copy.14
Async XLA Ops:
  1.3 0.7 copy-start.1
  108.6 1.9 %copy-start = (f32[64,64]{1,0:T(8,128)S(1)}, f32[64,64]{1,0:T(8,128)}, u32[]{:S(2)}) copy-start(f32[64,64]{1,0:T(8,128)} %get-tuple-element.9) | copy-start | bytes 49156
